TPU v7x, 32 devices: a whole 2x2x4 slice. The times are simulated.
32 devices in a mesh: groups: 2 (over y), context: 4 (over z), tensor: 4 (over x, core).
Axes of the slice: x: 2, y: 2, z: 4, core: 2. Of those that a mesh axis runs over, the one named last changes fastest.
Arguments:
- inputs: bfloat16 [4096, 1024], P(('groups', 'context')), parts along dimension 0, may hold values from -6 to 6
- frame_valid: int32 [4096], P(('groups', 'context')), parts along dimension 0, may hold values from 0 to 1, as said below
- norm1_gain: float32 [1024], replicated, may hold values from 0.1 to 1.9
- w_query: bfloat16 [1024, 1024], P(None, 'tensor')
- w_key: bfloat16 [1024, 1024], P(None, 'tensor')
- w_value: bfloat16 [1024, 1024], P(None, 'tensor'), may hold values from -0.1875 to 0.1875
- w_out: bfloat16 [1024, 1024], P('tensor'), may hold values from -0.1875 to 0.1875
- norm2_gain: float32 [1024], replicated, may hold values from 0.1 to 1.9
- w_point1: bfloat16 [2, 1024, 1024], P(None, None, 'tensor'), may hold values from -0.1875 to 0.1875
- w_depth: float32 [31, 1024], P(None, 'tensor'), may hold values from -1.5 to 1.5
- bn_scale: float32 [1024], P('tensor'), may hold values from 0.1 to 1.9
- bn_shift: float32 [1024], P('tensor'), may hold values from -1 to 1
- w_point2: bfloat16 [1024, 1024], P('tensor'), may hold values from -0.1875 to 0.1875
Outputs:
- output: bfloat16 [4096, 1024], P(('groups', 'context', 'tensor')), parts along dimension 0
There are 2 independent parts, one for each index of `groups`. A program takes and returns all parts, laid end to end along the dimension named above; an argument that names none is the same for every part. Nothing has to cross between parts.
Inputs may be any that keep to these rules, and one draw needn't show every extreme that they name: `frame_valid`: the transcript frames form a prefix of the window of at least 1024 frames, followed by at least one padded frame.
All inputs are finite; a program needn't handle non-finite values.
Results may differ from a plain program's by a relative error of at most 0.0095.
Values may be sent and summed in bfloat16 or wider, within the bound.
A program may use at most 64 MiB of HBM per device.

v0:
```python
import math
import jax
import jax.numpy as jnp
from jax import lax
from jax.sharding import PartitionSpec as P

HD = 64
NEG = -1e30


def with_halo(block, sides, width):
    for axis, dim in sides:
        count = lax.axis_size(axis)
        forward = [(i, i + 1) for i in range(count - 1)]
        backward = [(target, source) for source, target in forward]
        low = lax.ppermute(
            lax.slice_in_dim(block, block.shape[dim] - width, None, axis=dim), axis, forward
        )
        high = lax.ppermute(lax.slice_in_dim(block, 0, width, axis=dim), axis, backward)
        block = jnp.concatenate([low, block, high], axis=dim)
    return block


def normalize(rows, gain):
    values = rows.astype(jnp.float32)
    center = jnp.mean(values, axis=-1, keepdims=True)
    spread = jnp.mean(jnp.square(values - center), axis=-1, keepdims=True)
    return ((values - center) * lax.rsqrt(spread + 1e-05) * gain).astype(jnp.bfloat16)


def local(
    inputs,
    frame_valid,
    norm1_gain,
    w_query,
    w_key,
    w_value,
    w_out,
    norm2_gain,
    w_point1,
    w_depth,
    bn_scale,
    bn_shift,
    w_point2,
):
    frames = inputs.shape[0]
    local_cols = w_query.shape[1]
    head_dim = HD
    heads_here = local_cols // head_dim
    scale = 1.0 / math.sqrt(head_dim)
    normed = normalize(inputs, norm1_gain)
    query = jnp.dot(normed, w_query, preferred_element_type=jnp.float32).astype(jnp.bfloat16)
    query = query.reshape(frames, heads_here, head_dim)
    keys = jnp.dot(normed, w_key, preferred_element_type=jnp.float32).astype(jnp.bfloat16)
    vals = jnp.dot(normed, w_value, preferred_element_type=jnp.float32).astype(jnp.bfloat16)

    def update(carry, key_blk, val_blk, valid_blk):
        run_max, run_sum, accum = carry
        rows = key_blk.shape[0]
        key_heads = key_blk.reshape(rows, heads_here, head_dim)
        val_heads = val_blk.reshape(rows, heads_here, head_dim)
        scores = (
            jnp.einsum("qhd,khd->hqk", query, key_heads, preferred_element_type=jnp.float32) * scale
        )
        live = (valid_blk > 0)[None, None, :]
        scores = jnp.where(live, scores, NEG)
        new_max = jnp.maximum(run_max, jnp.max(scores, axis=-1))
        weights = jnp.where(live, jnp.exp(scores - new_max[:, :, None]), 0.0)
        factor = jnp.exp(run_max - new_max)
        run_sum = run_sum * factor + jnp.sum(weights, axis=-1)
        mixed = jnp.einsum(
            "hqk,khd->qhd",
            weights.astype(jnp.bfloat16),
            val_heads,
            preferred_element_type=jnp.float32,
        )
        accum = accum * jnp.repeat(factor.T, head_dim, axis=1) + mixed.reshape(frames, local_cols)
        return (new_max, run_sum, accum)

    def visit(carry, key_blk, val_blk, valid_blk):
        return update(carry, key_blk, val_blk, valid_blk)

    start_state = (
        jnp.full((heads_here, frames), NEG, jnp.float32),
        jnp.zeros((heads_here, frames), jnp.float32),
        jnp.zeros((frames, local_cols), jnp.float32),
    )
    carry = start_state
    key_part = lax.all_gather(keys, "context", axis=0, tiled=True)
    val_part = lax.all_gather(vals, "context", axis=0, tiled=True)
    valid_part = lax.all_gather(frame_valid, "context", axis=0, tiled=True)
    rows = key_part.shape[0]
    shards = max(rows // frames, 1)
    group = math.gcd(shards, max(1536 // frames, 1))
    blocks = shards // group
    block_rows = rows // blocks

    def advance(state, items):
        return (visit(state, items[0], items[1], items[2]), None)

    stacked = (
        key_part.reshape(blocks, block_rows, local_cols),
        val_part.reshape(blocks, block_rows, local_cols),
        valid_part.reshape(blocks, block_rows),
    )
    carry, unused = lax.scan(advance, carry, stacked)
    run_max, run_sum, accum = carry
    attended = (accum / jnp.repeat(run_sum.T, head_dim, axis=1)).astype(jnp.bfloat16)
    share = frames // lax.axis_size("tensor")
    first_row = lax.axis_index("tensor") * share
    total = lax.psum(jnp.dot(attended, w_out, preferred_element_type=jnp.float32), "tensor")
    residual = (inputs.astype(jnp.float32) + total).astype(jnp.bfloat16)
    normed_two = normalize(residual, norm2_gain)
    residual_rows = lax.dynamic_slice_in_dim(residual, first_row, share, 0)
    value_half = jnp.dot(normed_two, w_point1[0], preferred_element_type=jnp.float32)
    gate_half = jnp.dot(normed_two, w_point1[1], preferred_element_type=jnp.float32)
    gated = jnp.where(
        (frame_valid > 0)[:, None], value_half * jax.nn.sigmoid(gate_half), 0.0
    ).astype(jnp.bfloat16)
    taps = w_depth.shape[0]
    half = (taps - 1) // 2
    padded = with_halo(gated, (("context", 0),), half)
    depth = jnp.zeros((frames, gated.shape[1]), jnp.float32)
    for tap in range(taps):
        depth = depth + padded[tap : tap + frames].astype(jnp.float32) * w_depth[tap]
    activated = jax.nn.silu(depth * bn_scale + bn_shift).astype(jnp.bfloat16)
    conv_rows = lax.psum_scatter(
        jnp.dot(activated, w_point2, preferred_element_type=jnp.float32).astype(jnp.bfloat16),
        "tensor",
        scatter_dimension=0,
        tiled=True,
    ).astype(jnp.float32)
    return (residual_rows.astype(jnp.float32) + conv_rows).astype(jnp.bfloat16)


def solution(mesh):
    placed = (
        P(("groups", "context"), None),
        P(("groups", "context")),
        P(),
        P(None, "tensor"),
        P(None, "tensor"),
        P(None, "tensor"),
        P("tensor", None),
        P(),
        P(None, None, "tensor"),
        P(None, "tensor"),
        P("tensor"),
        P("tensor"),
        P("tensor", None),
    )
    return jax.shard_map(
        local,
        mesh=mesh,
        in_specs=placed,
        out_specs=P(("groups", "context", "tensor"), None),
        check_vma=False,
    )
```

profile of v0, /device:TPU:0, one launch (start us, length us, event | category | flops | bytes accessed | tf_op | source)
XLA Modules:
  0.0 218.2 jit_solution(7202695658550756041)
XLA Ops:
  12.5 13.7 %all-gather = s32[4,1,512]{2,1,0:T(1,128)S(1)} all-gather(s32[1,1,512]{2,1,0:T(1,128)S(1)} %bitcast.111), channel_id=1, replica_groups=mesh['groups'=2,'context'=4,'tensor'=4] {'context'}, dimensions={0}, use_global_device_ids=true | all-gather | bytes 10240 | tf_op jit(solution)/shard_map/all_gather | solution.py:91
  26.2 1.7 convolution_convert_fusion.2
  27.9 14.0 %all-gather.4.cloned.1.call-done = bf16[2048,256]{1,0:T(8,128)(2,1)} async-done(((bf16[512,256]{1,0:T(8,128)(2,1)}), bf16[2048,256]{1,0:T(8,128)(2,1)}) %all-gather.4.cloned.1.call-update) | async-done | bytes 1048592 | tf_op jit(solution)/shard_map/all_gather | solution.py:89
  41.9 29.0 %all-gather.6.cloned.1.call-done = bf16[2048,256]{1,0:T(8,128)(2,1)} async-done(((bf16[512,256]{1,0:T(8,128)(2,1)}), bf16[2048,256]{1,0:T(8,128)(2,1)}) %all-gather.6.cloned.1.call-update) | async-done | bytes 1048592 | tf_op jit(solution)/shard_map/all_gather | solution.py:90
  70.9 44.4 %while.15 = (s32[]{:T(128)}, f32[4,512]{1,0:T(4,128)S(1)}, f32[4,512]{1,0:T(4,128)S(1)}, f32[512,256]{0,1:T(8,128)S(1)}, s32[4,512]{1,0:T(4,128)S(1)}, /*index=5...) while((s32[]{:T(128)}, f32[4,512]{1,0:T(4,128)S(1)}, ...), condition=%wide.region_5.6_spmd.clone, body=%wide.region_2.5_spmd.clone.sunk | while | flops 282472960 | bytes 17698944 | solution.py:106
  72.2 2.9 %bitcast_reduce_fusion.2 = (f32[4,512]{1,0:T(4,128)S(1)}, f32[4,512,512]{2,1,0:T(8,128)}) fusion(pred[512]{0:T(512)(128)(4,1)S(1)} %compare_reduce_fusion.2, bf16[512,4,64]{0,2,1:T(8,128)(2,1)S(1)} %bitcast.104, bf16[512,4,64]{0,2,1:T(8,128)(2,1)S(1)} %get-tuple-element.237), kind=kOutput, calls=%fused_computation.1.clone.1 | convolution fusion | flops 137361408 | bytes 4727296 | tf_op jit(solution)/shard_map/while/body/eval_jaxpr/qhd,khd->hqk/dot_general | solution.py:63
  75.1 3.3 %fusion.96 = f32[4,512]{1,0:T(4,128)S(1)} fusion(f32[4,512,512]{2,1,0:T(8,128)} %get-tuple-element.208, f32[4,512]{1,0:T(4,128)S(1)} %get-tuple-element.232, pred[512]{0:T(512)(128)(4,1)S(1)} %compare_reduce_fusion.2), kind=kLoop, calls=%fused_computation.6.clone.1 | loop fusion | flops 5240832 | bytes 4211200 | tf_op jit(solution)/shard_map/while/body/eval_jaxpr/reduce_sum | solution.py:70
  78.6 3.3 %fusion.98 = f32[4,64,512]{2,1,0:T(8,128)S(1)} fusion(bf16[512,4,64]{0,2,1:T(8,128)(2,1)S(1)} %bitcast.106, f32[4,512,512]{2,1,0:T(8,128)} %get-tuple-element.208, f32[4,512]{1,0:T(4,128)S(1)} %get-tuple-element.232, pred[512]{0:T(512)(128)(4,1)S(1)} %compare_reduce_fusion.2), kind=kOutput, calls=%fused_computation.7.clone.1 | convolution fusion | flops 139460608 | bytes 4989440 | tf_op jit(solution)/shard_map/while/body/eval_jaxpr/hqk,khd->qhd/dot_general | solution.py:71
  83.3 2.9 %bitcast_reduce_fusion.2 = (f32[4,512]{1,0:T(4,128)S(1)}, f32[4,512,512]{2,1,0:T(8,128)}) fusion(pred[512]{0:T(512)(128)(4,1)S(1)} %compare_reduce_fusion.2, bf16[512,4,64]{0,2,1:T(8,128)(2,1)S(1)} %bitcast.104, bf16[512,4,64]{0,2,1:T(8,128)(2,1)S(1)} %get-tuple-element.237), kind=kOutput, calls=%fused_computation.1.clone.1 | convolution fusion | flops 137361408 | bytes 4727296 | tf_op jit(solution)/shard_map/while/body/eval_jaxpr/qhd,khd->hqk/dot_general | solution.py:63
  86.2 3.3 %fusion.96 = f32[4,512]{1,0:T(4,128)S(1)} fusion(f32[4,512,512]{2,1,0:T(8,128)} %get-tuple-element.208, f32[4,512]{1,0:T(4,128)S(1)} %get-tuple-element.232, pred[512]{0:T(512)(128)(4,1)S(1)} %compare_reduce_fusion.2), kind=kLoop, calls=%fused_computation.6.clone.1 | loop fusion | flops 5240832 | bytes 4211200 | tf_op jit(solution)/shard_map/while/body/eval_jaxpr/reduce_sum | solution.py:70
  89.7 3.3 %fusion.98 = f32[4,64,512]{2,1,0:T(8,128)S(1)} fusion(bf16[512,4,64]{0,2,1:T(8,128)(2,1)S(1)} %bitcast.106, f32[4,512,512]{2,1,0:T(8,128)} %get-tuple-element.208, f32[4,512]{1,0:T(4,128)S(1)} %get-tuple-element.232, pred[512]{0:T(512)(128)(4,1)S(1)} %compare_reduce_fusion.2), kind=kOutput, calls=%fused_computation.7.clone.1 | convolution fusion | flops 139460608 | bytes 4989440 | tf_op jit(solution)/shard_map/while/body/eval_jaxpr/hqk,khd->qhd/dot_general | solution.py:71
  94.4 2.9 %bitcast_reduce_fusion.2 = (f32[4,512]{1,0:T(4,128)S(1)}, f32[4,512,512]{2,1,0:T(8,128)}) fusion(pred[512]{0:T(512)(128)(4,1)S(1)} %compare_reduce_fusion.2, bf16[512,4,64]{0,2,1:T(8,128)(2,1)S(1)} %bitcast.104, bf16[512,4,64]{0,2,1:T(8,128)(2,1)S(1)} %get-tuple-element.237), kind=kOutput, calls=%fused_computation.1.clone.1 | convolution fusion | flops 137361408 | bytes 4727296 | tf_op jit(solution)/shard_map/while/body/eval_jaxpr/qhd,khd->hqk/dot_general | solution.py:63
  97.3 3.3 %fusion.96 = f32[4,512]{1,0:T(4,128)S(1)} fusion(f32[4,512,512]{2,1,0:T(8,128)} %get-tuple-element.208, f32[4,512]{1,0:T(4,128)S(1)} %get-tuple-element.232, pred[512]{0:T(512)(128)(4,1)S(1)} %compare_reduce_fusion.2), kind=kLoop, calls=%fused_computation.6.clone.1 | loop fusion | flops 5240832 | bytes 4211200 | tf_op jit(solution)/shard_map/while/body/eval_jaxpr/reduce_sum | solution.py:70
  100.8 3.3 %fusion.98 = f32[4,64,512]{2,1,0:T(8,128)S(1)} fusion(bf16[512,4,64]{0,2,1:T(8,128)(2,1)S(1)} %bitcast.106, f32[4,512,512]{2,1,0:T(8,128)} %get-tuple-element.208, f32[4,512]{1,0:T(4,128)S(1)} %get-tuple-element.232, pred[512]{0:T(512)(128)(4,1)S(1)} %compare_reduce_fusion.2), kind=kOutput, calls=%fused_computation.7.clone.1 | convolution fusion | flops 139460608 | bytes 4989440 | tf_op jit(solution)/shard_map/while/body/eval_jaxpr/hqk,khd->qhd/dot_general | solution.py:71
  105.5 2.9 %bitcast_reduce_fusion.2 = (f32[4,512]{1,0:T(4,128)S(1)}, f32[4,512,512]{2,1,0:T(8,128)}) fusion(pred[512]{0:T(512)(128)(4,1)S(1)} %compare_reduce_fusion.2, bf16[512,4,64]{0,2,1:T(8,128)(2,1)S(1)} %bitcast.104, bf16[512,4,64]{0,2,1:T(8,128)(2,1)S(1)} %get-tuple-element.237), kind=kOutput, calls=%fused_computation.1.clone.1 | convolution fusion | flops 137361408 | bytes 4727296 | tf_op jit(solution)/shard_map/while/body/eval_jaxpr/qhd,khd->hqk/dot_general | solution.py:63
  108.4 3.3 %fusion.96 = f32[4,512]{1,0:T(4,128)S(1)} fusion(f32[4,512,512]{2,1,0:T(8,128)} %get-tuple-element.208, f32[4,512]{1,0:T(4,128)S(1)} %get-tuple-element.232, pred[512]{0:T(512)(128)(4,1)S(1)} %compare_reduce_fusion.2), kind=kLoop, calls=%fused_computation.6.clone.1 | loop fusion | flops 5240832 | bytes 4211200 | tf_op jit(solution)/shard_map/while/body/eval_jaxpr/reduce_sum | solution.py:70
  111.9 3.3 %fusion.98 = f32[4,64,512]{2,1,0:T(8,128)S(1)} fusion(bf16[512,4,64]{0,2,1:T(8,128)(2,1)S(1)} %bitcast.106, f32[4,512,512]{2,1,0:T(8,128)} %get-tuple-element.208, f32[4,512]{1,0:T(4,128)S(1)} %get-tuple-element.232, pred[512]{0:T(512)(128)(4,1)S(1)} %compare_reduce_fusion.2), kind=kOutput, calls=%fused_computation.7.clone.1 | convolution fusion | flops 139460608 | bytes 4989440 | tf_op jit(solution)/shard_map/while/body/eval_jaxpr/hqk,khd->qhd/dot_general | solution.py:71
  115.4 1.8 fusion.73
  117.4 50.9 %all-reduce.2.cloned.1.call-done = f32[512,1024]{1,0:T(8,128)} async-done(((f32[512,1024]{1,0:T(8,128)}), f32[512,1024]{1,0:T(8,128)}) %all-reduce.2.cloned.1.call-update) | async-done | bytes 2097168 | tf_op jit(solution)/shard_map/psum | solution.py:111
  168.3 2.0 convert_reduce_fusion.1
  173.2 4.5 %collective-permute-start = (bf16[15,256]{1,0:T(8,128)(2,1)S(1)}, bf16[15,256]{1,0:T(8,128)(2,1)S(1)}, u32[]{:S(2)}, u32[]{:S(2)}) collective-permute-start(bf16[15,256]{1,0:T(8,128)(2,1)S(1)} %get-tuple-element.117), channel_id=1, source_target_pairs={{0,4},{4,8},{8,12},{1,5},{5,9},{9,13},{2,6},{6,10},{10,14},{3,7},{... | collective-permute-start | bytes 23048 | tf_op jit(solution)/shard_map/ppermute | solution.py:16
  179.1 4.9 %convolution_convert_fusion = bf16[512,1024]{1,0:T(8,128)(2,1)} fusion(bf16[256,1024]{1,0:T(8,128)(2,1)S(1)} %copy-done.7, bf16[512,256]{1,0:T(8,128)(2,1)S(1)} %fusion.28, bf16[15,256]{1,0:T(8,128)(2,1)S(1)} %collective-permute-done.1, bf16[15,256]{1,0:T(8,128)(2,1)S(1)} %collective-permute-done, f32[256]{0:T(256)S(1)} %copy-done.10, ...), kind=kOutput, calls=%fused_computation.67 | convolution fusion | flops 293732352 | bytes 1884160 | tf_op jit(solution)/shard_map/dot_general | solution.py:128
  184.0 26.0 %reduce-scatter.2.cloned.1.call-done = bf16[128,1024]{1,0:T(8,128)(2,1)} async-done(((bf16[512,1024]{1,0:T(8,128)(2,1)}), bf16[128,1024]{1,0:T(8,128)(2,1)}) %reduce-scatter.2.cloned.1.call-update) | async-done | bytes 262160 | tf_op jit(solution)/shard_map/reduce_scatter | solution.py:127
  209.9 1.7 add_convert_fusion
  (87 shorter events, 16.5 us)
Async XLA Ops:
  6.5 108.9 %copy-start = (bf16[256,1024]{1,0:T(8,128)(2,1)S(1)}, bf16[256,1024]{1,0:T(8,128)(2,1)}, u32[]{:S(2)}) copy-start(bf16[256,1024]{1,0:T(8,128)(2,1)} %param.21) | copy-start | bytes 1572868
  6.5 3.3 %copy-start.1 = (bf16[512,1024]{1,0:T(8,128)(2,1)S(1)}, bf16[512,1024]{1,0:T(8,128)(2,1)}, u32[]{:S(2)}) copy-start(bf16[512,1024]{1,0:T(8,128)(2,1)} %param.15) | copy-start | bytes 3145732
  6.5 3.3 %copy-start.5 = (bf16[1024,256]{1,0:T(8,128)(2,1)S(1)}, bf16[1024,256]{1,0:T(8,128)(2,1)}, u32[]{:S(2)}) copy-start(bf16[1024,256]{1,0:T(8,128)(2,1)} %param.19) | copy-start | bytes 1572868
  6.5 3.3 %copy-start.8 = (f32[1024]{0:T(1024)S(1)}, f32[1024]{0:T(1024)}, u32[]{:S(2)}) copy-start(f32[1024]{0:T(1024)} %param.17) | copy-start | bytes 12292
  6.5 35.4 %all-gather.4.cloned.1.call-start = ((), (), s32[]{:S(2)}) async-start(), calls=%async_computation.1 | async-start | bytes 1310720 | tf_op jit(solution)/shard_map/all_gather | solution.py:89
  9.8 1.4 copy-start.6
  11.1 1.4 copy-start.3
  11.1 59.8 %all-gather.6.cloned.1.call-start = ((), (), s32[]{:S(2)}) async-start(), calls=%async_computation.2 | async-start | bytes 1310720 | tf_op jit(solution)/shard_map/all_gather | solution.py:90
  12.4 155.9 %all-reduce.2.cloned.1.call-start = ((), (), s32[]{:S(2)}) async-start(), calls=%async_computation.3 | async-start | bytes 4194304 | tf_op jit(solution)/shard_map/psum | solution.py:111
  115.4 1.9 copy-start.2
  117.2 92.7 %reduce-scatter.2.cloned.1.call-start = ((), (), s32[]{:S(2)}) async-start(), calls=%async_computation.4 | async-start | bytes 1310720 | tf_op jit(solution)/shard_map/reduce_scatter | solution.py:127
  117.3 53.4 %copy-start.9 = (f32[1024]{0:T(1024)S(1)}, f32[1024]{0:T(1024)}, u32[]{:S(2)}) copy-start(f32[1024]{0:T(1024)} %param.22) | copy-start | bytes 12292
  168.3 2.4 %copy-start.4 = (bf16[2,1024,256]{2,1,0:T(8,128)(2,1)S(1)}, bf16[2,1024,256]{2,1,0:T(8,128)(2,1)}, u32[]{:S(2)}) copy-start(bf16[2,1024,256]{2,1,0:T(8,128)(2,1)} %param.23) | copy-start | bytes 3145732
  171.3 7.8 %copy-start.7 = (bf16[256,1024]{1,0:T(8,128)(2,1)S(1)}, bf16[256,1024]{1,0:T(8,128)(2,1)}, u32[]{:S(2)}) copy-start(bf16[256,1024]{1,0:T(8,128)(2,1)} %param.27) | copy-start | bytes 1572868
  171.3 7.8 %copy-start.10 = (f32[256]{0:T(256)S(1)}, f32[256]{0:T(256)}, u32[]{:S(2)}) copy-start(f32[256]{0:T(256)} %param.26) | copy-start | bytes 3076
  171.3 7.8 %copy-start.11 = (f32[256]{0:T(256)S(1)}, f32[256]{0:T(256)}, u32[]{:S(2)}) copy-start(f32[256]{0:T(256)} %param.25) | copy-start | bytes 3076
  171.9 5.9 %collective-permute-start.1 = (bf16[15,256]{1,0:T(8,128)(2,1)S(1)}, bf16[15,256]{1,0:T(8,128)(2,1)S(1)}, u32[]{:S(2)}, u32[]{:S(2)}) collective-permute-start(bf16[15,256]{1,0:T(8,128)(2,1)S(1)} %get-tuple-element.118), channel_id=1, source_target_pairs={{4,0},{8,4},{12,8},{5,1},{9,5},{13,9},{6,2},{10,6},{14,10},{7,3},{... | collective-permute-start | bytes 23048 | tf_op jit(solution)/shard_map/ppermute | solution.py:19
  173.2 5.9 %collective-permute-start = (bf16[15,256]{1,0:T(8,128)(2,1)S(1)}, bf16[15,256]{1,0:T(8,128)(2,1)S(1)}, u32[]{:S(2)}, u32[]{:S(2)}) collective-permute-start(bf16[15,256]{1,0:T(8,128)(2,1)S(1)} %get-tuple-element.117), channel_id=1, source_target_pairs={{0,4},{4,8},{8,12},{1,5},{5,9},{9,13},{2,6},{6,10},{10,14},{3,7},{... | collective-permute-start | bytes 23048 | tf_op jit(solution)/shard_map/ppermute | solution.py:16
Sparse Core Ops, SparseCore 0:
  11.2 30.6 all-gather.3
  43.5 27.3 all-gather.5
  117.4 50.8 all-reduce.1
  184.1 25.8 reduce-scatter.1
where the time goes:
time: 219 us; the launch traced here: 218 us
  waiting for transfers between devices  121 us (55%)
  matrix products  36.7 us (17%)
  other arithmetic  21.4 us (10%)
  blocking collectives  13.7 us (6%)
  between operations  13.4 us (6%)
  starting transfers between devices  6 us (3%)
  local copies, waits for them, and re-layouts  5.5 us (3%)
    psum x1, waiting for transfers between devices, local(): lax.psum(jnp.dot(attended, w_out, preferred_element_type=jnp.float32), 't...  50.9 us
    all_gather x1, waiting for transfers between devices, local(): val_part = lax.all_gather(vals, 'context', axis=0, tiled=True)  29 us
    reduce_scatter x1, waiting for transfers between devices, local(): lax.psum_scatter(jnp.dot(activated, w_point2, preferred_element_type=jnp....  26 us
    all_gather x1, waiting for transfers between devices, local(): key_part = lax.all_gather(keys, 'context', axis=0, tiled=True)  14 us
    all_gather x1, blocking collectives, local(): valid_part = lax.all_gather(frame_valid, 'context', axis=0, tiled=True)  13.7 us
    dot_general x4, matrix products, update(): jnp.einsum('hqk,khd->qhd', weights.astype(jnp.bfloat16), val_heads, prefe...  13.1 us
    reduce_sum x4, other arithmetic, update(): run_sum = run_sum * factor + jnp.sum(weights, axis=-1)  13.1 us
    dot_general x4, matrix products, update(): jnp.einsum('qhd,khd->hqk', query, key_heads, preferred_element_type=jnp.f...  11.6 us
  transfers between devices with their start and end apart: 6, of which 5 were waited for; matrix products, arithmetic and copies ran while one was open for 1% of the time, Pallas kernels for 0%

commit v1 on v0

--- a/solution.py
+++ b/solution.py
@@ -3,6 +3,7 @@
 import jax.numpy as jnp
 from jax import lax
 from jax.sharding import PartitionSpec as P
+from jax.lax import axis_index, axis_size, ppermute
 
 HD = 64
 NEG = -1e30
@@ -86,7 +87,15 @@
         jnp.zeros((frames, local_cols), jnp.float32),
     )
     carry = start_state
-    key_part = lax.all_gather(keys, "context", axis=0, tiled=True)
+    n_chips = axis_size("context")
+    even = sorted(((pp, (pp + 1) % n_chips) for pp in range(n_chips)))
+    passed = keys
+    shelf = [passed]
+    for idx in range(1, n_chips):
+        passed = ppermute(passed, "context", perm=even)
+        shelf.insert(0, passed)
+    kept_arr = jnp.concatenate(shelf, axis=0)
+    key_part = jnp.roll(kept_arr, (axis_index("context") + 1) * keys.shape[0], axis=0)
     val_part = lax.all_gather(vals, "context", axis=0, tiled=True)
     valid_part = lax.all_gather(frame_valid, "context", axis=0, tiled=True)
     rows = key_part.shape[0]

time: 219 us -> 206 us (0.941)
  waiting for transfers between devices: 121 us -> 105 us
  starting transfers between devices: 6 us -> 9.09 us
    all_gather x1, waiting for transfers between devices: 29 us -> 4.59 us  [local(): val_part = lax.all_gather(vals, 'context', axis=0, tiled=True)]
    ppermute x0 -> x3, waiting for transfers between devices: none -> 21.8 us  [local(): passed = ppermute(passed, 'context', perm=even)]
    all_gather x1 -> x0, waiting for transfers between devices: 14 us -> none  [local(): key_part = lax.all_gather(keys, 'context', axis=0, tiled=True)]
    ppermute x0 -> x3, starting transfers between devices: none -> 3.14 us  [local(): passed = ppermute(passed, 'context', perm=even)]
  transfers between devices with their start and end apart: 6 -> 8, of which waited for: 5 -> 6; matrix products, arithmetic and copies ran while one was open for 1% -> 2% of each run, Pallas kernels for 0% -> 0%
where the time goes in v1:
time: 206 us
  waiting for transfers between devices  105 us (51%)
  matrix products  36 us (17%)
  other arithmetic  21.5 us (10%)
  blocking collectives  13.9 us (7%)
  between operations  13.4 us (7%)
  starting transfers between devices  9.09 us (4%)
  local copies, waits for them, and re-layouts  6.74 us (3%)
    psum x1, waiting for transfers between devices, local(): lax.psum(jnp.dot(attended, w_out, preferred_element_type=jnp.float32), 't...  50.9 us
    reduce_scatter x1, waiting for transfers between devices, local(): lax.psum_scatter(jnp.dot(activated, w_point2, preferred_element_type=jnp....  26 us
    ppermute x3, waiting for transfers between devices, local(): passed = ppermute(passed, 'context', perm=even)  21.8 us
    all_gather x1, blocking collectives, local(): valid_part = lax.all_gather(frame_valid, 'context', axis=0, tiled=True)  13.9 us
    dot_general x4, matrix products, update(): jnp.einsum('hqk,khd->qhd', weights.astype(jnp.bfloat16), val_heads, prefe...  13.1 us
    reduce_sum x4, other arithmetic, update(): run_sum = run_sum * factor + jnp.sum(weights, axis=-1)  13.1 us
    dot_general x4, matrix products, update(): jnp.einsum('qhd,khd->hqk', query, key_heads, preferred_element_type=jnp.f...  11.6 us
    dynamic_slice x12, local copies, waits for them, and re-layouts, local(): carry, unused = lax.scan(advance, carry, stacked)  5.39 us
  transfers between devices with their start and end apart: 8, of which 6 were waited for; matrix products, arithmetic and copies ran while one was open for 2% of the time, Pallas kernels for 0%

profile of v1, /device:TPU:0, one launch (start us, length us, event | category | flops | bytes accessed | tf_op | source)
XLA Modules:
  0.0 205.5 jit_solution(6507195544647511607)
XLA Ops:
  10.4 3.1 %collective-permute-start = (bf16[512,256]{1,0:T(8,128)(2,1)S(1)}, bf16[512,256]{1,0:T(8,128)(2,1)S(1)}, u32[]{:S(2)}, u32[]{:S(2)}) collective-permute-start(bf16[512,256]{1,0:T(8,128)(2,1)S(1)} %convolution_convert_fusion.3), channel_id=1, source_target_pairs={{0,4},{4,8},{8,12},{12,0},{1,5},{5,9},{9,13},{13,1},{2,6},{6,10},{... | collective-permute-start | bytes 786440 | tf_op jit(solution)/shard_map/ppermute | solution.py:95
  13.5 8.3 %collective-permute-done = bf16[512,256]{1,0:T(8,128)(2,1)S(1)} collective-permute-done((bf16[512,256]{1,0:T(8,128)(2,1)S(1)}, bf16[512,256]{1,0:T(8,128)(2,1)S(1)}, u32[]{:S(2)}, u32[]{:S(2)}) %collective-permute-start) | collective-permute-done | bytes 262176 | tf_op jit(solution)/shard_map/ppermute | solution.py:95
  23.2 13.9 %all-gather = s32[4,1,512]{2,1,0:T(1,128)S(1)} all-gather(s32[1,1,512]{2,1,0:T(1,128)S(1)} %bitcast.111), channel_id=1, replica_groups=mesh['groups'=2,'context'=4,'tensor'=4] {'context'}, dimensions={0}, use_global_device_ids=true | all-gather | bytes 10240 | tf_op jit(solution)/shard_map/all_gather | solution.py:100
  39.0 13.4 %collective-permute-done.2 = bf16[512,256]{1,0:T(8,128)(2,1)S(1)} collective-permute-done((bf16[512,256]{1,0:T(8,128)(2,1)S(1)}, bf16[512,256]{1,0:T(8,128)(2,1)S(1)}, u32[]{:S(2)}, u32[]{:S(2)}) %collective-permute-start.2) | collective-permute-done | bytes 262176 | tf_op jit(solution)/shard_map/ppermute | solution.py:95
  53.7 4.6 %all-gather.3.cloned.1.call-done = bf16[2048,256]{1,0:T(8,128)(2,1)} async-done(((bf16[512,256]{1,0:T(8,128)(2,1)}), bf16[2048,256]{1,0:T(8,128)(2,1)}) %all-gather.3.cloned.1.call-update) | async-done | bytes 1048592 | tf_op jit(solution)/shard_map/all_gather | solution.py:99
  58.3 44.4 %while.15 = (s32[]{:T(128)}, f32[4,512]{1,0:T(4,128)S(1)}, f32[4,512]{1,0:T(4,128)S(1)}, f32[512,256]{0,1:T(8,128)S(1)}, s32[4,512]{1,0:T(4,128)S(1)}, /*index=5...) while((s32[]{:T(128)}, f32[4,512]{1,0:T(4,128)S(1)}, ...), condition=%wide.region_5.6_spmd.clone, body=%wide.region_2.5_spmd.clone.sunk | while | flops 282472960 | bytes 17698944 | solution.py:115
  59.5 2.9 %bitcast_reduce_fusion.2 = (f32[4,512]{1,0:T(4,128)S(1)}, f32[4,512,512]{2,1,0:T(8,128)}) fusion(pred[512]{0:T(512)(128)(4,1)S(1)} %compare_reduce_fusion.2, bf16[512,4,64]{0,2,1:T(8,128)(2,1)S(1)} %bitcast.104, bf16[512,4,64]{0,2,1:T(8,128)(2,1)S(1)} %get-tuple-element.245), kind=kOutput, calls=%fused_computation.1.clone.1 | convolution fusion | flops 137361408 | bytes 4727296 | tf_op jit(solution)/shard_map/while/body/eval_jaxpr/qhd,khd->hqk/dot_general | solution.py:64
  62.5 3.3 %fusion.96 = f32[4,512]{1,0:T(4,128)S(1)} fusion(f32[4,512,512]{2,1,0:T(8,128)} %get-tuple-element.216, f32[4,512]{1,0:T(4,128)S(1)} %get-tuple-element.240, pred[512]{0:T(512)(128)(4,1)S(1)} %compare_reduce_fusion.2), kind=kLoop, calls=%fused_computation.6.clone.1 | loop fusion | flops 5240832 | bytes 4211200 | tf_op jit(solution)/shard_map/while/body/eval_jaxpr/reduce_sum | solution.py:71
  65.9 3.3 %fusion.98 = f32[4,64,512]{2,1,0:T(8,128)S(1)} fusion(bf16[512,4,64]{0,2,1:T(8,128)(2,1)S(1)} %bitcast.106, f32[4,512,512]{2,1,0:T(8,128)} %get-tuple-element.216, f32[4,512]{1,0:T(4,128)S(1)} %get-tuple-element.240, pred[512]{0:T(512)(128)(4,1)S(1)} %compare_reduce_fusion.2), kind=kOutput, calls=%fused_computation.7.clone.1 | convolution fusion | flops 139460608 | bytes 4989440 | tf_op jit(solution)/shard_map/while/body/eval_jaxpr/hqk,khd->qhd/dot_general | solution.py:72
  70.6 2.9 %bitcast_reduce_fusion.2 = (f32[4,512]{1,0:T(4,128)S(1)}, f32[4,512,512]{2,1,0:T(8,128)}) fusion(pred[512]{0:T(512)(128)(4,1)S(1)} %compare_reduce_fusion.2, bf16[512,4,64]{0,2,1:T(8,128)(2,1)S(1)} %bitcast.104, bf16[512,4,64]{0,2,1:T(8,128)(2,1)S(1)} %get-tuple-element.245), kind=kOutput, calls=%fused_computation.1.clone.1 | convolution fusion | flops 137361408 | bytes 4727296 | tf_op jit(solution)/shard_map/while/body/eval_jaxpr/qhd,khd->hqk/dot_general | solution.py:64
  73.6 3.3 %fusion.96 = f32[4,512]{1,0:T(4,128)S(1)} fusion(f32[4,512,512]{2,1,0:T(8,128)} %get-tuple-element.216, f32[4,512]{1,0:T(4,128)S(1)} %get-tuple-element.240, pred[512]{0:T(512)(128)(4,1)S(1)} %compare_reduce_fusion.2), kind=kLoop, calls=%fused_computation.6.clone.1 | loop fusion | flops 5240832 | bytes 4211200 | tf_op jit(solution)/shard_map/while/body/eval_jaxpr/reduce_sum | solution.py:71
  77.0 3.3 %fusion.98 = f32[4,64,512]{2,1,0:T(8,128)S(1)} fusion(bf16[512,4,64]{0,2,1:T(8,128)(2,1)S(1)} %bitcast.106, f32[4,512,512]{2,1,0:T(8,128)} %get-tuple-element.216, f32[4,512]{1,0:T(4,128)S(1)} %get-tuple-element.240, pred[512]{0:T(512)(128)(4,1)S(1)} %compare_reduce_fusion.2), kind=kOutput, calls=%fused_computation.7.clone.1 | convolution fusion | flops 139460608 | bytes 4989440 | tf_op jit(solution)/shard_map/while/body/eval_jaxpr/hqk,khd->qhd/dot_general | solution.py:72
  81.7 2.9 %bitcast_reduce_fusion.2 = (f32[4,512]{1,0:T(4,128)S(1)}, f32[4,512,512]{2,1,0:T(8,128)}) fusion(pred[512]{0:T(512)(128)(4,1)S(1)} %compare_reduce_fusion.2, bf16[512,4,64]{0,2,1:T(8,128)(2,1)S(1)} %bitcast.104, bf16[512,4,64]{0,2,1:T(8,128)(2,1)S(1)} %get-tuple-element.245), kind=kOutput, calls=%fused_computation.1.clone.1 | convolution fusion | flops 137361408 | bytes 4727296 | tf_op jit(solution)/shard_map/while/body/eval_jaxpr/qhd,khd->hqk/dot_general | solution.py:64
  84.7 3.3 %fusion.96 = f32[4,512]{1,0:T(4,128)S(1)} fusion(f32[4,512,512]{2,1,0:T(8,128)} %get-tuple-element.216, f32[4,512]{1,0:T(4,128)S(1)} %get-tuple-element.240, pred[512]{0:T(512)(128)(4,1)S(1)} %compare_reduce_fusion.2), kind=kLoop, calls=%fused_computation.6.clone.1 | loop fusion | flops 5240832 | bytes 4211200 | tf_op jit(solution)/shard_map/while/body/eval_jaxpr/reduce_sum | solution.py:71
  88.1 3.3 %fusion.98 = f32[4,64,512]{2,1,0:T(8,128)S(1)} fusion(bf16[512,4,64]{0,2,1:T(8,128)(2,1)S(1)} %bitcast.106, f32[4,512,512]{2,1,0:T(8,128)} %get-tuple-element.216, f32[4,512]{1,0:T(4,128)S(1)} %get-tuple-element.240, pred[512]{0:T(512)(128)(4,1)S(1)} %compare_reduce_fusion.2), kind=kOutput, calls=%fused_computation.7.clone.1 | convolution fusion | flops 139460608 | bytes 4989440 | tf_op jit(solution)/shard_map/while/body/eval_jaxpr/hqk,khd->qhd/dot_general | solution.py:72
  92.8 2.9 %bitcast_reduce_fusion.2 = (f32[4,512]{1,0:T(4,128)S(1)}, f32[4,512,512]{2,1,0:T(8,128)}) fusion(pred[512]{0:T(512)(128)(4,1)S(1)} %compare_reduce_fusion.2, bf16[512,4,64]{0,2,1:T(8,128)(2,1)S(1)} %bitcast.104, bf16[512,4,64]{0,2,1:T(8,128)(2,1)S(1)} %get-tuple-element.245), kind=kOutput, calls=%fused_computation.1.clone.1 | convolution fusion | flops 137361408 | bytes 4727296 | tf_op jit(solution)/shard_map/while/body/eval_jaxpr/qhd,khd->hqk/dot_general | solution.py:64
  95.8 3.3 %fusion.96 = f32[4,512]{1,0:T(4,128)S(1)} fusion(f32[4,512,512]{2,1,0:T(8,128)} %get-tuple-element.216, f32[4,512]{1,0:T(4,128)S(1)} %get-tuple-element.240, pred[512]{0:T(512)(128)(4,1)S(1)} %compare_reduce_fusion.2), kind=kLoop, calls=%fused_computation.6.clone.1 | loop fusion | flops 5240832 | bytes 4211200 | tf_op jit(solution)/shard_map/while/body/eval_jaxpr/reduce_sum | solution.py:71
  99.2 3.3 %fusion.98 = f32[4,64,512]{2,1,0:T(8,128)S(1)} fusion(bf16[512,4,64]{0,2,1:T(8,128)(2,1)S(1)} %bitcast.106, f32[4,512,512]{2,1,0:T(8,128)} %get-tuple-element.216, f32[4,512]{1,0:T(4,128)S(1)} %get-tuple-element.240, pred[512]{0:T(512)(128)(4,1)S(1)} %compare_reduce_fusion.2), kind=kOutput, calls=%fused_computation.7.clone.1 | convolution fusion | flops 139460608 | bytes 4989440 | tf_op jit(solution)/shard_map/while/body/eval_jaxpr/hqk,khd->qhd/dot_general | solution.py:72
  102.8 1.8 fusion.73
  104.7 50.9 %all-reduce.2.cloned.1.call-done = f32[512,1024]{1,0:T(8,128)} async-done(((f32[512,1024]{1,0:T(8,128)}), f32[512,1024]{1,0:T(8,128)}) %all-reduce.2.cloned.1.call-update) | async-done | bytes 2097168 | tf_op jit(solution)/shard_map/psum | solution.py:120
  155.6 2.0 convert_reduce_fusion.1
  160.5 4.5 %collective-permute-start.3 = (bf16[15,256]{1,0:T(8,128)(2,1)S(1)}, bf16[15,256]{1,0:T(8,128)(2,1)S(1)}, u32[]{:S(2)}, u32[]{:S(2)}) collective-permute-start(bf16[15,256]{1,0:T(8,128)(2,1)S(1)} %get-tuple-element.125), channel_id=1, source_target_pairs={{0,4},{4,8},{8,12},{1,5},{5,9},{9,13},{2,6},{6,10},{10,14},{3,7},{... | collective-permute-start | bytes 23048 | tf_op jit(solution)/shard_map/ppermute | solution.py:17
  166.4 4.9 %convolution_convert_fusion = bf16[512,1024]{1,0:T(8,128)(2,1)} fusion(bf16[256,1024]{1,0:T(8,128)(2,1)S(1)} %copy-done.7, bf16[512,256]{1,0:T(8,128)(2,1)S(1)} %fusion.28, bf16[15,256]{1,0:T(8,128)(2,1)S(1)} %collective-permute-done.4, bf16[15,256]{1,0:T(8,128)(2,1)S(1)} %collective-permute-done.3, f32[256]{0:T(256)S(1)} %copy-done.10, ...), kind=kOutput, calls=%fused_computation.67 | convolution fusion | flops 293732352 | bytes 1884160 | tf_op jit(solution)/shard_map/dot_general | solution.py:137
  171.3 26.0 %reduce-scatter.2.cloned.1.call-done = bf16[128,1024]{1,0:T(8,128)(2,1)} async-done(((bf16[512,1024]{1,0:T(8,128)(2,1)}), bf16[128,1024]{1,0:T(8,128)(2,1)}) %reduce-scatter.2.cloned.1.call-update) | async-done | bytes 262160 | tf_op jit(solution)/shard_map/reduce_scatter | solution.py:136
  (99 shorter events, 20.6 us)
Async XLA Ops:
  6.5 96.2 %copy-start = (bf16[256,1024]{1,0:T(8,128)(2,1)S(1)}, bf16[256,1024]{1,0:T(8,128)(2,1)}, u32[]{:S(2)}) copy-start(bf16[256,1024]{1,0:T(8,128)(2,1)} %param.21) | copy-start | bytes 1572868
  6.5 3.3 %copy-start.1 = (bf16[512,1024]{1,0:T(8,128)(2,1)S(1)}, bf16[512,1024]{1,0:T(8,128)(2,1)}, u32[]{:S(2)}) copy-start(bf16[512,1024]{1,0:T(8,128)(2,1)} %param.15) | copy-start | bytes 3145732
  6.5 3.4 %copy-start.5 = (bf16[1024,256]{1,0:T(8,128)(2,1)S(1)}, bf16[1024,256]{1,0:T(8,128)(2,1)}, u32[]{:S(2)}) copy-start(bf16[1024,256]{1,0:T(8,128)(2,1)} %param.19) | copy-start | bytes 1572868
  6.5 3.4 %copy-start.8 = (f32[1024]{0:T(1024)S(1)}, f32[1024]{0:T(1024)}, u32[]{:S(2)}) copy-start(f32[1024]{0:T(1024)} %param.17) | copy-start | bytes 12292
  6.5 51.7 %all-gather.3.cloned.1.call-start = ((), (), s32[]{:S(2)}) async-start(), calls=%async_computation.1 | async-start | bytes 1310720 | tf_op jit(solution)/shard_map/all_gather | solution.py:99
  8.2 13.7 %copy-start.6 = (bf16[1024,256]{1,0:T(8,128)(2,1)S(1)}, bf16[1024,256]{1,0:T(8,128)(2,1)}, u32[]{:S(2)}) copy-start(bf16[1024,256]{1,0:T(8,128)(2,1)} %param.20) | copy-start | bytes 1572868
  10.4 12.8 %copy-start.3 = (s32[512]{0:T(512)S(1)}, s32[512]{0:T(512)}, u32[]{:S(2)}) copy-start(s32[512]{0:T(512)} %param.16) | copy-start | bytes 6148
  10.4 11.4 %collective-permute-start = (bf16[512,256]{1,0:T(8,128)(2,1)S(1)}, bf16[512,256]{1,0:T(8,128)(2,1)S(1)}, u32[]{:S(2)}, u32[]{:S(2)}) collective-permute-start(bf16[512,256]{1,0:T(8,128)(2,1)S(1)} %convolution_convert_fusion.3), channel_id=1, source_target_pairs={{0,4},{4,8},{8,12},{12,0},{1,5},{5,9},{9,13},{13,1},{2,6},{6,10},{... | collective-permute-start | bytes 786440 | tf_op jit(solution)/shard_map/ppermute | solution.py:95
  21.9 15.3 %collective-permute-start.1 = (bf16[512,256]{1,0:T(8,128)(2,1)S(1)}, bf16[512,256]{1,0:T(8,128)(2,1)S(1)}, u32[]{:S(2)}, u32[]{:S(2)}) collective-permute-start(bf16[512,256]{1,0:T(8,128)(2,1)S(1)} %collective-permute-done), channel_id=1, source_target_pairs={{0,4},{4,8},{8,12},{12,0},{1,5},{5,9},{9,13},{13,1},{2,6},{6,10},{... | collective-permute-start | bytes 786440 | tf_op jit(solution)/shard_map/ppermute | solution.py:95
  23.1 132.5 %all-reduce.2.cloned.1.call-start = ((), (), s32[]{:S(2)}) async-start(), calls=%async_computation.2 | async-start | bytes 4194304 | tf_op jit(solution)/shard_map/psum | solution.py:120
  37.2 15.2 %collective-permute-start.2 = (bf16[512,256]{1,0:T(8,128)(2,1)S(1)}, bf16[512,256]{1,0:T(8,128)(2,1)S(1)}, u32[]{:S(2)}, u32[]{:S(2)}) collective-permute-start(bf16[512,256]{1,0:T(8,128)(2,1)S(1)} %collective-permute-done.1), channel_id=1, source_target_pairs={{0,4},{4,8},{8,12},{12,0},{1,5},{5,9},{9,13},{13,1},{2,6},{6,10},{... | collective-permute-start | bytes 786440 | tf_op jit(solution)/shard_map/ppermute | solution.py:95
  102.8 1.9 copy-start.2
  104.6 92.7 %reduce-scatter.2.cloned.1.call-start = ((), (), s32[]{:S(2)}) async-start(), calls=%async_computation.3 | async-start | bytes 1310720 | tf_op jit(solution)/shard_map/reduce_scatter | solution.py:136
  104.7 53.4 %copy-start.9 = (f32[1024]{0:T(1024)S(1)}, f32[1024]{0:T(1024)}, u32[]{:S(2)}) copy-start(f32[1024]{0:T(1024)} %param.22) | copy-start | bytes 12292
  155.6 2.4 %copy-start.4 = (bf16[2,1024,256]{2,1,0:T(8,128)(2,1)S(1)}, bf16[2,1024,256]{2,1,0:T(8,128)(2,1)}, u32[]{:S(2)}) copy-start(bf16[2,1024,256]{2,1,0:T(8,128)(2,1)} %param.23) | copy-start | bytes 3145732
  158.6 7.8 %copy-start.7 = (bf16[256,1024]{1,0:T(8,128)(2,1)S(1)}, bf16[256,1024]{1,0:T(8,128)(2,1)}, u32[]{:S(2)}) copy-start(bf16[256,1024]{1,0:T(8,128)(2,1)} %param.27) | copy-start | bytes 1572868
  158.6 7.8 %copy-start.10 = (f32[256]{0:T(256)S(1)}, f32[256]{0:T(256)}, u32[]{:S(2)}) copy-start(f32[256]{0:T(256)} %param.26) | copy-start | bytes 3076
  158.6 7.8 %copy-start.11 = (f32[256]{0:T(256)S(1)}, f32[256]{0:T(256)}, u32[]{:S(2)}) copy-start(f32[256]{0:T(256)} %param.25) | copy-start | bytes 3076
  159.2 5.9 %collective-permute-start.4 = (bf16[15,256]{1,0:T(8,128)(2,1)S(1)}, bf16[15,256]{1,0:T(8,128)(2,1)S(1)}, u32[]{:S(2)}, u32[]{:S(2)}) collective-permute-start(bf16[15,256]{1,0:T(8,128)(2,1)S(1)} %get-tuple-element.126), channel_id=1, source_target_pairs={{4,0},{8,4},{12,8},{5,1},{9,5},{13,9},{6,2},{10,6},{14,10},{7,3},{... | collective-permute-start | bytes 23048 | tf_op jit(solution)/shard_map/ppermute | solution.py:20
  160.5 5.9 %collective-permute-start.3 = (bf16[15,256]{1,0:T(8,128)(2,1)S(1)}, bf16[15,256]{1,0:T(8,128)(2,1)S(1)}, u32[]{:S(2)}, u32[]{:S(2)}) collective-permute-start(bf16[15,256]{1,0:T(8,128)(2,1)S(1)} %get-tuple-element.125), channel_id=1, source_target_pairs={{0,4},{4,8},{8,12},{1,5},{5,9},{9,13},{2,6},{6,10},{10,14},{3,7},{... | collective-permute-start | bytes 23048 | tf_op jit(solution)/shard_map/ppermute | solution.py:17
Sparse Core Ops, SparseCore 0:
  23.2 35.0 all-gather.2
  104.7 50.8 all-reduce.1
  171.4 25.8 reduce-scatter.1
